TPU v7x, 512 devices: a whole 4x4x16 slice. The times are simulated.
512 devices in a mesh: dp: 16 (over x, z_lo), ctx: 32 (over z_hi, y, core).
Axes of the slice: x: 4, y: 4, z: 16 (z_hi: 4, z_lo: 4; z = z_hi * 4 + z_lo), core: 2. Of those that a mesh axis runs over, the one named last changes fastest.
Arguments:
- query_rows: bfloat16 [65536, 512], P(('dp', 'ctx')), may hold values from -6 to 6
- key_rows: bfloat16 [65536, 512], P(('dp', 'ctx')), may hold values from -6 to 6
- value_rows: bfloat16 [65536, 512], P(('dp', 'ctx')), may hold values from -6 to 6
- gate_rows: bfloat16 [65536, 512], P(('dp', 'ctx')), may hold values from -6 to 6
- positives: bfloat16 [65536, 512], P(('dp', 'ctx')), may hold values from -0.8984375 to 0.8984375
- negatives: bfloat16 [512, 512], P('dp'), may hold values from -18 to 18
- history_lengths: int32 [16, 4], P('dp'), may hold values from 1 to 2048, 4096 in all within a row
Outputs:
- grad_queries: bfloat16 [65536, 512], P(('dp', 'ctx'))
- grad_gates: bfloat16 [65536, 512], P(('dp', 'ctx'))
- grad_negatives: float32 [512, 512], P(('dp', 'ctx'))
Inputs may be any that keep to these rules, and one draw needn't show every extreme that they name: `history_lengths`: each row sums to 4096; its longest history is exactly 2048.
All inputs are finite; a program needn't handle non-finite values.
Results may differ from a plain program's by a relative error of at most 0.022.
The roundings to bfloat16 on the way count: a program that leaves them out, or rounds other values in their place, can miss the bound.
Values may be sent and summed in bfloat16 or wider, within the bound.
A program may use at most 64 MiB of HBM per device.

v0:
```python
import math

import jax
import jax.numpy as jnp
from jax import lax
from jax.sharding import PartitionSpec as P

HEADS = 4


eps = 1e-05


def segment_of(places, bounds):
    return jnp.sum((places[:, None] >= bounds[None, :]).astype(jnp.int32), axis=1)


def scores_for(q_heads, k_block, q_places, user_ids, k_start, user_ends):
    key_count = k_block.shape[0]
    k_places = k_start + jnp.arange(key_count, dtype=jnp.int32)
    k_users = segment_of(k_places, user_ends)
    allowed = (user_ids[:, None] == k_users[None, :]) & (k_places[None, :] <= q_places[:, None])
    k_heads = k_block.reshape(key_count, q_heads.shape[1], q_heads.shape[2])
    score_scale = q_heads.shape[2] ** (-0.5)
    logits = (
        jnp.einsum("rhd,khd->hrk", q_heads, k_heads, preferred_element_type=jnp.float32)
        * score_scale
    )
    return (logits, allowed[None], k_heads, score_scale)


def sweep(running, k_all, v_all, k_start, adder):
    key_count = k_all.shape[0]
    block_rows = math.gcd(key_count, 1024)
    block_total = key_count // block_rows
    low_block = 0

    def advance(block_index, partial_sum):
        offset = block_index * block_rows
        k_block = lax.dynamic_slice_in_dim(k_all, offset, block_rows, 0)
        v_block = lax.dynamic_slice_in_dim(v_all, offset, block_rows, 0)
        return adder(partial_sum, k_block, v_block, k_start + offset)

    return lax.fori_loop(low_block, block_total, advance, running)


def on_device(query_rows, key_rows, value_rows, gate_rows, positives, negatives, history_lengths):
    row_count, feature_count = query_rows.shape
    head_size = feature_count // HEADS
    lengths_here = history_lengths[0]
    user_ends = jnp.cumsum(lengths_here)
    q_places = lax.axis_index("ctx") * row_count + jnp.arange(row_count, dtype=jnp.int32)
    user_ids = segment_of(q_places, user_ends)
    q_heads = query_rows.reshape(row_count, HEADS, head_size)
    all_negatives = lax.all_gather(negatives, "dp", axis=0, tiled=True)

    def add_forward(partial_sum, k_block, v_block, k_start):
        logits, allowed, k_heads, score_scale = scores_for(
            q_heads, k_block, q_places, user_ids, k_start, user_ends
        )
        weights = jnp.where(allowed, jax.nn.silu(logits), 0.0).astype(jnp.bfloat16)
        v_heads = v_block.reshape(k_heads.shape)
        return partial_sum + jnp.einsum(
            "hrk,khd->rhd", weights, v_heads, preferred_element_type=jnp.float32
        )

    empty_heads = jnp.zeros((row_count, HEADS, head_size), jnp.float32)
    k_all, v_all = (
        lax.all_gather(key_rows, "ctx", axis=0, tiled=True),
        lax.all_gather(value_rows, "ctx", axis=0, tiled=True),
    )
    attended = sweep(empty_heads, k_all, v_all, 0, add_forward)
    attended = attended.reshape(row_count, feature_count)
    inverse_rms = lax.rsqrt(jnp.mean(attended * attended, axis=1, keepdims=True) + eps)
    normed = attended * inverse_rms
    gates_wide = gate_rows.astype(jnp.float32)
    positive_wide = positives.astype(jnp.float32)
    hidden_b = (normed * gates_wide).astype(jnp.bfloat16)
    own_logit = jnp.sum(hidden_b.astype(jnp.float32) * positive_wide, axis=1)
    other_logits = jnp.einsum(
        "re,ne->rn", hidden_b, all_negatives, preferred_element_type=jnp.float32
    )
    largest = jnp.maximum(own_logit, jnp.max(other_logits, axis=1))
    exp_own = jnp.exp(own_logit - largest)
    exp_others = jnp.exp(other_logits - largest[:, None])
    partition = exp_own + jnp.sum(exp_others, axis=1)
    probs_b = (exp_others / partition[:, None]).astype(jnp.bfloat16)
    own_prob = exp_own / partition
    d_hidden = (own_prob - 1.0)[:, None] * positive_wide + jnp.dot(
        probs_b, all_negatives, preferred_element_type=jnp.float32
    )
    grad_gates = (d_hidden * normed).astype(jnp.bfloat16)
    d_normed = d_hidden * gates_wide
    d_attended = inverse_rms * (
        d_normed - normed * jnp.mean(d_normed * normed, axis=1, keepdims=True)
    )
    d_heads = d_attended.astype(jnp.bfloat16).reshape(row_count, HEADS, head_size)

    def add_backward(partial_sum, k_block, v_block, k_start):
        logits, allowed, k_heads, score_scale = scores_for(
            q_heads, k_block, q_places, user_ids, k_start, user_ends
        )
        v_heads = v_block.reshape(k_heads.shape)
        d_weights = jnp.einsum("rhd,khd->hrk", d_heads, v_heads, preferred_element_type=jnp.float32)
        sigmoid_values = jax.nn.sigmoid(logits)
        d_logits = jnp.where(
            allowed,
            d_weights * sigmoid_values * (1.0 + logits * (1.0 - sigmoid_values)) * score_scale,
            0.0,
        ).astype(jnp.bfloat16)
        return partial_sum + jnp.einsum(
            "hrk,khd->rhd", d_logits, k_heads, preferred_element_type=jnp.float32
        )

    grad_heads = sweep(empty_heads, k_all, v_all, 0, add_backward)
    grad_queries = grad_heads.reshape(row_count, feature_count).astype(jnp.bfloat16)
    grad_negatives = lax.psum_scatter(
        jnp.einsum("rn,re->ne", probs_b, hidden_b, preferred_element_type=jnp.float32),
        ("dp", "ctx"),
        scatter_dimension=0,
        tiled=True,
    )
    return (grad_queries, grad_gates, grad_negatives)


def solution(mesh):
    placed = (
        P(("dp", "ctx"), None),
        P(("dp", "ctx"), None),
        P(("dp", "ctx"), None),
        P(("dp", "ctx"), None),
        P(("dp", "ctx"), None),
        P("dp", None),
        P("dp", None),
    )
    return jax.shard_map(
        on_device,
        mesh=mesh,
        in_specs=placed,
        out_specs=(P(("dp", "ctx"), None), P(("dp", "ctx"), None), P(("dp", "ctx"), None)),
        check_vma=False,
    )
```

profile of v0, /device:TPU:1, one launch (start us, length us, event | category | flops | bytes accessed | tf_op | source)
XLA Modules:
  0.0 708.4 jit_solution(11888991892297615315)
XLA Ops:
  7.2 1.7 copy.57
  8.9 1.7 copy.58
  10.7 0.8 reduce-window.8
  11.5 1.0 copy.59
  12.6 0.1 copy.60
  12.8 47.1 %all_gather.11 = bf16[512,512]{1,0:T(8,128)(2,1)S(1)} all-gather(bf16[32,512]{1,0:T(8,128)(2,1)} %param.16), channel_id=1, replica_groups=mesh['dp'=16,'ctx'=32] {'dp'}, dimensions={0}, use_global_device_ids=true | all-gather | bytes 557056 | tf_op jit(solution)/shard_map/all_gather | solution.py:55
  59.9 61.4 %all-gather.3.cloned.1.call-done = bf16[4096,512]{0,1:T(8,128)(2,1)} async-done(((bf16[128,512]{0,1:T(8,128)(2,1)}), bf16[4096,512]{0,1:T(8,128)(2,1)}) %all-gather.3.cloned.1.call-update) | async-done | bytes 4194320 | tf_op jit(solution)/shard_map/all_gather | solution.py:69
  121.3 101.6 %all-gather.5.cloned.1.call-done = bf16[4096,512]{0,1:T(8,128)(2,1)} async-done(((bf16[128,512]{0,1:T(8,128)(2,1)}), bf16[4096,512]{0,1:T(8,128)(2,1)}) %all-gather.5.cloned.1.call-update) | async-done | bytes 4194320 | tf_op jit(solution)/shard_map/all_gather | solution.py:70
  222.9 14.1 %while.28 = (s32[]{:T(128)}, f32[128,4,128]{0,2,1:T(8,128)S(1)}, bf16[4096,512]{0,1:T(8,128)(2,1)}, s32[128]{0:T(128)S(1)}, s32[4]{0:T(128)S(1)}, /*index=5*/bf1...) while((s32[]{:T(128)}, f32[128,4,128]{0,2,1:T(8,128)S(1)}, ...), condition=%wide.region_4.5_spmd.clone, body=%wide.region_2.4_spmd.clone.sunk | while | flops 272642176 | bytes 7231177 | solution.py:44
  222.9 1.8 constant_dynamic-slice_fusion.7
  224.7 0.3 compare_and_fusion.4
  225.1 1.3 fusion.73
  226.4 1.7 constant_dynamic-slice_fusion.7
  228.2 0.3 compare_and_fusion.4
  228.6 1.3 fusion.73
  229.9 1.7 constant_dynamic-slice_fusion.7
  231.7 0.3 compare_and_fusion.4
  232.1 1.3 fusion.73
  233.4 1.7 constant_dynamic-slice_fusion.7
  235.2 0.3 compare_and_fusion.4
  235.6 1.3 fusion.73
  237.2 0.2 fusion.39
  237.4 0.4 fusion.45
  237.8 0.2 fusion.40
  238.0 1.4 fusion.43
  239.4 0.4 multiply_reduce_fusion
  239.8 0.8 multiply_convert_fusion
  240.6 23.3 %while.29 = (s32[]{:T(128)}, f32[128,4,128]{0,2,1:T(8,128)}, bf16[4096,512]{0,1:T(8,128)(2,1)}, s32[128]{0:T(128)S(1)}, s32[4]{0:T(128)S(1)}, /*index=5*/bf16[40...) while((s32[]{:T(128)}, f32[128,4,128]{0,2,1:T(8,128)}, ...), condition=%wide.region_12.13_spmd.clone, body=%wide.region_10.12_spmd.clone.sunk | while | flops 409481344 | bytes 11556561 | solution.py:44
  240.7 1.7 constant_dynamic-slice_fusion.8
  242.4 0.5 fusion.79
  243.0 0.3 compare_and_fusion.5
  243.4 2.4 fusion.80
  245.8 1.7 constant_dynamic-slice_fusion.8
  247.5 0.5 fusion.79
  248.1 0.3 compare_and_fusion.5
  248.5 3.3 fusion.80
  251.8 1.7 constant_dynamic-slice_fusion.8
  253.6 0.5 fusion.79
  254.2 0.3 compare_and_fusion.5
  254.6 3.3 fusion.80
  257.9 1.7 constant_dynamic-slice_fusion.8
  259.6 0.5 fusion.79
  260.3 0.3 compare_and_fusion.5
  260.6 3.3 fusion.80
  264.0 1.0 convert_element_type.65
  264.9 0.8 copy.71
  265.7 434.8 %all-reduce.3.cloned.1.call-done = f32[512,512]{1,0:T(8,128)} async-done(((f32[512,512]{1,0:T(8,128)}), f32[512,512]{1,0:T(8,128)}) %all-reduce.3.cloned.1.call-update) | async-done | bytes 1048592
  700.5 1.3 constant_dynamic-slice_fusion.4
  (45 shorter events, 1.3 us)
Async XLA Ops:
  7.2 114.1 %all-gather.3.cloned.1.call-start = ((), (), s32[]{:S(2)}) async-start(), calls=%async_computation | async-start | bytes 4325376 | tf_op jit(solution)/shard_map/all_gather | solution.py:69
  8.9 214.0 %all-gather.5.cloned.1.call-start = ((), (), s32[]{:S(2)}) async-start(), calls=%async_computation.1 | async-start | bytes 4325376 | tf_op jit(solution)/shard_map/all_gather | solution.py:70
  10.6 689.9 %all-reduce.3.cloned.1.call-start = ((), (), s32[]{:S(2)}) async-start(), calls=%async_computation.2 | async-start | bytes 2097152
  222.9 14.3 %copy-start = (bf16[128,512]{1,0:T(8,128)(2,1)S(1)}, bf16[128,512]{1,0:T(8,128)(2,1)}, u32[]{:S(2)}) copy-start(bf16[128,512]{1,0:T(8,128)(2,1)} %param.14) | copy-start | bytes 393220
  222.9 14.3 %copy-start.1 = (bf16[128,512]{1,0:T(8,128)(2,1)S(1)}, bf16[128,512]{1,0:T(8,128)(2,1)}, u32[]{:S(2)}) copy-start(bf16[128,512]{1,0:T(8,128)(2,1)} %param.15) | copy-start | bytes 393220
Sparse Core Ops, SparseCore 0:
  11.6 109.6 all-gather.2
  124.9 97.9 all-gather.4
  239.5 460.9 all-reduce.2
where the time goes:
time: 709 us; the launch traced here: 708 us
  waiting for transfers between devices  598 us (84%)
  blocking collectives  47.1 us (7%)
  matrix products  21.9 us (3%)
  local copies, waits for them, and re-layouts  20.5 us (3%)
  between operations  13.9 us (2%)
    unnamed x4, waiting for transfers between devices  435 us
    all_gather x1, waiting for transfers between devices, on_device(): lax.all_gather(value_rows, 'ctx', axis=0, tiled=True)  102 us
    all_gather x1, waiting for transfers between devices, on_device(): lax.all_gather(key_rows, 'ctx', axis=0, tiled=True)  61.4 us
    all_gather x1, blocking collectives, on_device(): all_negatives = lax.all_gather(negatives, 'dp', axis=0, tiled=True)  47.1 us
  transfers between devices with their start and end apart: 3, of which 3 were waited for; matrix products, arithmetic and copies ran while one was open for 4% of the time, Pallas kernels for 0%

commit v1 on v0

v1 whole, which is shorter than its diff:
```python
import jax
import jax.numpy as jnp
from jax import lax
from jax.experimental import pallas as pl
from jax.experimental.pallas import tpu as pltpu
from jax.sharding import PartitionSpec as P

HEADS = 4
HEAD = 128
WIDTH = 512
ROWS = 128
QUARTER = 32
SCALE = HEAD ** (-0.5)
EPS = 1e-05
MESH = pl.DeviceIdType.MESH

ORDER_1 = (0, 1, 2, 3)
ORDER_2 = (0, 2, 6, 4, 7, 5, 1, 3)
ORDER_3 = (0, 1, 4, 5, 2, 6, 3, 7)


def packed(order):
    return sum(code << (3 * place) for place, code in enumerate(order))


def pick(h, values):
    out = jnp.int32(values[3])
    for index in (2, 1, 0):
        out = jnp.where(h == index, jnp.int32(values[index]), out)
    return out


def dot_last(a, b):
    return lax.dot_general(a, b, (((1,), (1,)), ((), ())), preferred_element_type=jnp.float32)


def dot_first(a, b):
    return lax.dot_general(a, b, (((0,), (0,)), ((), ())), preferred_element_type=jnp.float32)


def dot(a, b):
    return jnp.dot(a, b, preferred_element_type=jnp.float32)


def kernel(
    lengths, q_ref, k_hbm, v_hbm, gate_ref, pos_ref, neg_ref,
    gq_out, gg_out, gn_out,
    kv, att, slope, negs_raw, negs, d_att, c_send, c_recv, own_half, xy_send, xy_recv, z_send, z_recv,
    local_sem, kv_recv, z_sem, y_sem, c_sem,
    nx_send, nx_recv, nl_send, nl_recv, ny_send, ny_recv, nc_send, nc_recv,
    rc_send, rc_recv, rxy_send, rxy_recv, rz_send, rz_recv,
):
    dp, ctx = lax.axis_index("dp"), lax.axis_index("ctx")
    x, l = dp // 4, dp % 4
    h, y, c = ctx // 8, (ctx // 2) % 4, ctx % 2
    z = h * 4 + l

    def device(x2, l2, h2, y2, c2):
        return (x2 * 4 + l2, (h2 * 4 + y2) * 2 + c2)

    sibling = device(x, l, h, y, 1 - c)

    def z_peer(k):
        z2 = (z + k) % 16
        return z2, device(x, z2 % 4, z2 // 4, y, c)

    def xy_peer(k):
        x2, y2 = (x + k // 4) % 4, (y + k % 4) % 4
        return x2 * 4 + y2, device(x2, l, h, y2, c)

    local = []
    for q in range(4):
        for kind, source in ((0, k_hbm), (1, v_hbm)):
            local.append(pltpu.make_async_copy(
                source.at[pl.ds(q * QUARTER, QUARTER)], kv.at[h, q, kind, y, c], local_sem.at[q * 2 + kind]))
    for copy in local:
        copy.start()

    barrier = pltpu.get_barrier_semaphore()
    pl.semaphore_signal(barrier, inc=1, device_id=sibling, device_id_type=MESH)
    for k in range(1, 16):
        pl.semaphore_signal(barrier, inc=1, device_id=z_peer(k)[1], device_id_type=MESH)
        pl.semaphore_signal(barrier, inc=1, device_id=xy_peer(k)[1], device_id_type=MESH)

    for y2 in range(4):
        @pl.when(y2 > y)
        def _():
            for q in range(4):
                kv[h, q, :, y2] = jnp.zeros((2, 2, QUARTER, WIDTH), jnp.bfloat16)

        @pl.when((h >= 2) & (y2 < y))
        def _():
            for q in range(4):
                kv[h - 2, q, :, y2] = jnp.zeros((2, 2, QUARTER, WIDTH), jnp.bfloat16)

    att[...] = jnp.zeros_like(att)
    for copy in local:
        copy.wait()
    pl.semaphore_wait(barrier, 31)

    def piece_copy(hb, q, y2, c2, send_sem, target):
        piece = kv.at[hb, q, :, y2, c2]
        return pltpu.make_async_remote_copy(
            src_ref=piece, dst_ref=piece, send_sem=send_sem, recv_sem=kv_recv.at[hb, q, y2, c2],
            device_id=target, device_id_type=MESH)

    def piece_arrived(hb, q, y2, c2):
        piece_copy(hb, q, y2, c2, z_sem.at[0, 0, 0], sibling).wait_recv()

    def forward(hb, q, kind):
        return piece_copy(hb, q, y, c, z_sem.at[0, kind, q], device(x, l, (h + 1) % 4, y, c))

    def backward(hb, q, kind):
        return piece_copy(hb, q, y, c, z_sem.at[1, kind, q], device(x, l, (h + 3) % 4, y, c))

    def sends_forward(q):
        return (h <= 2) if q != 1 else ((h == 0) | (h == 2))

    def sends_backward(q):
        return {0: h < 0, 1: h == 1, 2: h <= 1, 3: h <= 1}[q]

    for q in range(4):
        pl.when(sends_forward(q))(lambda q=q: forward(h, q, 0).start())
        if q > 0:
            pl.when(sends_backward(q))(lambda q=q: backward(h, q, 0).start())

    def neg_x(k):
        part = neg_ref.at[pl.ds(c * 16, 16)]
        return pltpu.make_async_remote_copy(
            src_ref=part, dst_ref=negs_raw.at[y, c, l], send_sem=nx_send.at[k - 1], recv_sem=nx_recv.at[0],
            device_id=device((x + k) % 4, l, h, y, c), device_id_type=MESH)

    def neg_z(k):
        part = negs_raw.at[y, c, l]
        l2 = (l + k) % 4
        z2 = (z + (k if k < 3 else 15)) % 16
        return pltpu.make_async_remote_copy(
            src_ref=part, dst_ref=part, send_sem=nl_send.at[k - 1], recv_sem=nl_recv.at[k - 1],
            device_id=device(x, l2, z2 // 4, y, c), device_id_type=MESH)

    def neg_z_arrived(k):
        part = negs_raw.at[y, c, (l + 4 - k) % 4]
        pltpu.make_async_remote_copy(
            src_ref=part, dst_ref=part, send_sem=nl_send.at[k - 1], recv_sem=nl_recv.at[k - 1],
            device_id=sibling, device_id_type=MESH).wait_recv()

    def neg_y(k):
        part = negs_raw.at[y, c]
        return pltpu.make_async_remote_copy(
            src_ref=part, dst_ref=part, send_sem=ny_send.at[k - 1], recv_sem=ny_recv.at[k - 1],
            device_id=device(x, l, h, (y + k) % 4, c), device_id_type=MESH)

    def neg_y_arrived(k):
        part = negs_raw.at[(y + 4 - k) % 4, c]
        pltpu.make_async_remote_copy(
            src_ref=part, dst_ref=part, send_sem=ny_send.at[k - 1], recv_sem=ny_recv.at[k - 1],
            device_id=sibling, device_id_type=MESH).wait_recv()

    def neg_c(c2):
        part = negs_raw.at[:, c2]
        return pltpu.make_async_remote_copy(
            src_ref=part, dst_ref=part, send_sem=nc_send.at[0], recv_sem=nc_recv.at[0],
            device_id=sibling, device_id_type=MESH)

    @pl.when(x == y)
    def _():
        for k in (1, 2, 3):
            neg_x(k).start()

    places = ctx * ROWS + lax.broadcasted_iota(jnp.int32, (ROWS, 1), 0)
    first = jnp.zeros((ROWS, 1), jnp.int32)
    user_end = jnp.int32(0)
    for user in range(4):
        user_end = user_end + lengths[0, user]
        first = jnp.where(places >= user_end, user_end, first)

    orders = pick(h, [0, packed(ORDER_1), packed(ORDER_2), packed(ORDER_3)])
    ranks = pick(h, [4, 8, 12, 12])

    def rank_of(e):
        code = lax.shift_right_logical(orders, 3 * jnp.maximum(e - 4, 0)) & 7
        back = jnp.where(e < 4, 0, 1 + code // 4)
        return back, jnp.where(e < 4, e, code % 4)

    def comes_from(back, y2):
        return (back == 1) | ((back == 0) & (y2 < y)) | ((back == 2) & (y2 > y))

    def goes_to(back, y2):
        return (back == 1) | ((back == 0) & (y2 > y)) | ((back == 2) & (y2 < y))

    def z_forwards(back, q):
        return ((h == 1) & (back == 1) & (q < 2)) | ((h == 2) & (back == 1) & (q == 0))

    def z_backwards(back, q):
        return (h == 3) & (back == 2) & (q == 1)

    def y_copy(e, hb, q, k):
        return piece_copy(hb, q, y, c, y_sem.at[e, k - 1], device(x, l, h, (y + k) % 4, c))

    def c_copy(e, hb, q, y2):
        return piece_copy(hb, q, y2, c, c_sem.at[e, y2], sibling)

    def transit(hb, q):
        piece_arrived(hb, q, y, c)
        backward(hb, q, 1).start()

    def column_event(e):
        back, q = rank_of(e)
        hb = h - back
        pl.when(back > 0)(lambda: piece_arrived(hb, q, y, c))
        pl.when(z_forwards(back, q))(lambda: forward(hb, q, 1).start())
        pl.when(z_backwards(back, q))(lambda: backward(hb, q, 1).start())
        for k in (1, 3, 2):
            pl.when(goes_to(back, (y + k) % 4))(lambda k=k: y_copy(e, hb, q, k).start())
        c_copy(e, hb, q, y).start()

    def row_event(e):
        back, q = rank_of(e)
        hb = h - back
        for k in (1, 3, 2):
            y2 = (y + k) % 4

            @pl.when(comes_from(back, y2))
            def _():
                piece_arrived(hb, q, y2, c)
                c_copy(e, hb, q, y2).start()

    def compute_event(e):
        back, q = rank_of(e)
        hb = h - back
        for k in range(4):
            y2 = (y + k) % 4
            pl.when(True if k == 0 else comes_from(back, y2))(lambda y2=y2: piece_arrived(hb, q, y2, 1 - c))
        at = lax.broadcasted_iota(jnp.int32, (ROWS, 8 * QUARTER), 1)
        k_places = hb * 1024 + q * QUARTER + (at // QUARTER) * ROWS + at % QUARTER
        allowed = (k_places >= first) & (k_places <= places)
        for head in range(HEADS):
            lanes = pl.ds(head * HEAD, HEAD)
            k_head = kv[hb, q, 0, :, :, :, lanes].reshape(8 * QUARTER, HEAD)
            v_head = kv[hb, q, 1, :, :, :, lanes].reshape(8 * QUARTER, HEAD)
            logits = dot_last(q_ref[:, lanes], k_head)
            sigmoid = 0.5 * jnp.tanh(logits * (0.5 * SCALE)) + 0.5
            silu = logits * SCALE * sigmoid
            weights = jnp.where(allowed, silu, 0.0).astype(jnp.bfloat16)
            slope[e, head] = jnp.where(allowed, (sigmoid + silu * (1.0 - sigmoid)) * SCALE, 0.0)
            att[:, lanes] += dot(weights, v_head)

    def step(e, carry):
        pl.when(e < ranks)(lambda: column_event(e))

        @pl.when(h == 3)
        def _():
            pl.when(e == 4)(lambda: transit(0, 2))
            pl.when(e == 5)(lambda: transit(0, 3))

        @pl.when(e == 2)
        def _():
            @pl.when(x != y)
            def _():
                part = negs_raw.at[y, c, l]
                pltpu.make_async_remote_copy(
                    src_ref=part, dst_ref=part, send_sem=nx_send.at[0], recv_sem=nx_recv.at[0],
                    device_id=sibling, device_id_type=MESH).wait_recv()

            @pl.when(x == y)
            def _():
                negs_raw[y, c, l] = neg_ref[pl.ds(pl.multiple_of(c * 16, 16), 16), :]

            for k in (1, 2, 3):
                neg_z(k).start()

        @pl.when(e == 4)
        def _():
            for k in (1, 2, 3):
                neg_z_arrived(k)
            for k in (1, 2, 3):
                neg_y(k).start()

        @pl.when(e == 5)
        def _():
            for k in (1, 2, 3):
                neg_y_arrived(k)
            neg_c(c).start()

        pl.when(e >= 2)(lambda: compute_event(e - 2))
        pl.when((e >= 1) & (e <= ranks))(lambda: row_event(e - 1))
        return carry

    @pl.when(h == 0)
    def _():
        lax.fori_loop(0, 6, step, 0)
        for q in (1, 2, 3):
            transit(1, q)

    @pl.when(h != 0)
    def _():
        lax.fori_loop(0, ranks + 2, step, 0)

    neg_c(1 - c).wait_recv()
    to = lax.broadcasted_iota(jnp.int32, (512, 512), 0)
    source = ((((to // 64) % 4 * 2 + (to // 8) % 2) * 4 + to % 4) * 16
              + (to // 4) % 2 * 8 + (to // 16) % 4 * 2 + to // 256)
    chosen = lax.broadcasted_iota(jnp.int32, (512, 512), 1) == source
    negs[...] = dot(
        jnp.where(chosen, 1.0, 0.0).astype(jnp.bfloat16), negs_raw[...].reshape(512, WIDTH)
    ).astype(jnp.bfloat16)

    attended = att[...]
    inverse_rms = lax.rsqrt(jnp.mean(attended * attended, axis=1, keepdims=True) + EPS)
    normed = attended * inverse_rms
    gates = gate_ref[...].astype(jnp.float32)
    positives = pos_ref[...].astype(jnp.float32)
    hidden = (normed * gates).astype(jnp.bfloat16)
    own_logit = jnp.sum(hidden.astype(jnp.float32) * positives, axis=1, keepdims=True)
    other_logits = dot_last(hidden, negs[...])
    largest = jnp.maximum(own_logit, jnp.max(other_logits, axis=1, keepdims=True))
    exp_own = jnp.exp(own_logit - largest)
    exp_others = jnp.exp(other_logits - largest)
    partition = exp_own + jnp.sum(exp_others, axis=1, keepdims=True)
    probs = (exp_others / partition).astype(jnp.bfloat16)
    own_prob = exp_own / partition

    low, high = probs[:, :256], probs[:, 256:]
    c_send[...] = dot_first(jnp.where(c == 0, high, low), hidden).astype(jnp.bfloat16)
    c_reduce = pltpu.make_async_remote_copy(
        src_ref=c_send, dst_ref=c_recv, send_sem=rc_send.at[0], recv_sem=rc_recv.at[0],
        device_id=sibling, device_id_type=MESH)
    c_reduce.start()
    own_half[...] = dot_first(jnp.where(c == 0, low, high), hidden)
    c_reduce.wait_recv()
    xy_send[...] = (own_half[...] + c_recv[...].astype(jnp.float32)).astype(jnp.bfloat16).reshape(16, 16, WIDTH)
    here = x * 4 + y

    def xy_copy(k):
        there, target = xy_peer(k)
        return pltpu.make_async_remote_copy(
            src_ref=xy_send.at[there], dst_ref=xy_recv.at[here], send_sem=rxy_send.at[k - 1],
            recv_sem=rxy_recv.at[k - 1], device_id=target, device_id_type=MESH)

    def xy_arrived(k):
        part = xy_recv.at[((x + 4 - k // 4) % 4) * 4 + (y + 4 - k % 4) % 4]
        pltpu.make_async_remote_copy(
            src_ref=part, dst_ref=part, send_sem=rxy_send.at[k - 1], recv_sem=rxy_recv.at[k - 1],
            device_id=sibling, device_id_type=MESH).wait_recv()

    for k in range(1, 16):
        xy_copy(k).start()
    xy_recv[here] = xy_send[here]

    d_hidden = (own_prob - 1.0) * positives + dot(probs, negs[...])
    gg_out[...] = (d_hidden * normed).astype(jnp.bfloat16)
    d_normed = d_hidden * gates
    d_att[...] = (
        inverse_rms * (d_normed - normed * jnp.mean(d_normed * normed, axis=1, keepdims=True))
    ).astype(jnp.bfloat16)

    att[...] = jnp.zeros_like(att)

    def back_step(e, carry):
        back, q = rank_of(e)
        hb = h - back
        for head in range(HEADS):
            lanes = pl.ds(head * HEAD, HEAD)
            k_head = kv[hb, q, 0, :, :, :, lanes].reshape(8 * QUARTER, HEAD)
            v_head = kv[hb, q, 1, :, :, :, lanes].reshape(8 * QUARTER, HEAD)
            d_weights = dot_last(d_att[:, lanes], v_head)
            d_scores = (d_weights * slope[e, head]).astype(jnp.bfloat16)
            att[:, lanes] += dot(d_scores, k_head)
        return carry

    lax.fori_loop(0, ranks, back_step, 0)

    for k in range(1, 16):
        xy_arrived(k)
    total = xy_recv[0].astype(jnp.float32)
    for k in range(1, 16):
        total = total + xy_recv[k].astype(jnp.float32)
    for row in range(16):
        for part in range(4):
            z_send[row, part:part + 1, :] = total[row:row + 1, part * 128:(part + 1) * 128]

    def z_copy(k):
        there, target = z_peer(k)
        return pltpu.make_async_remote_copy(
            src_ref=z_send.at[there], dst_ref=z_recv.at[z], send_sem=rz_send.at[k - 1],
            recv_sem=rz_recv.at[k - 1], device_id=target, device_id_type=MESH)

    def z_arrived(k):
        part = z_recv.at[(z + 16 - k) % 16]
        pltpu.make_async_remote_copy(
            src_ref=part, dst_ref=part, send_sem=rz_send.at[k - 1], recv_sem=rz_recv.at[k - 1],
            device_id=sibling, device_id_type=MESH).wait_recv()

    for k in (8, 7, 9, 6, 10, 5, 11, 4, 12, 3, 13, 2, 14, 1, 15):
        z_copy(k).start()
    z_recv[z] = z_send[z]
    gq_out[...] = att[...].astype(jnp.bfloat16)

    for q in range(4):
        pl.when(sends_forward(q))(lambda q=q: forward(h, q, 0).wait_send())
        if q > 0:
            pl.when(sends_backward(q))(lambda q=q: backward(h, q, 0).wait_send())

    @pl.when(x == y)
    def _():
        for k in (1, 2, 3):
            neg_x(k).wait_send()

    for k in (1, 2, 3):
        neg_z(k).wait_send()
        neg_y(k).wait_send()
    neg_c(c).wait_send()

    @pl.when(h == 0)
    def _():
        for q in (1, 2, 3):
            backward(1, q, 1).wait_send()

    @pl.when(h == 3)
    def _():
        for q in (2, 3):
            backward(0, q, 1).wait_send()

    def drain(e, carry):
        back, q = rank_of(e)
        hb = h - back
        pl.when(z_forwards(back, q))(lambda: forward(hb, q, 1).wait_send())
        pl.when(z_backwards(back, q))(lambda: backward(hb, q, 1).wait_send())
        for k in (1, 2, 3):
            y2 = (y + k) % 4
            pl.when(goes_to(back, y2))(lambda k=k: y_copy(e, hb, q, k).wait_send())
            pl.when(comes_from(back, y2))(lambda y2=y2: c_copy(e, hb, q, y2).wait_send())
        c_copy(e, hb, q, y).wait_send()
        return carry

    lax.fori_loop(0, ranks, drain, 0)
    c_reduce.wait_send()
    for k in range(1, 16):
        xy_copy(k).wait_send()

    for k in range(1, 16):
        z_arrived(k)
    grad = z_recv[0]
    for k in range(1, 16):
        grad = grad + z_recv[k]
    for part in range(4):
        gn_out[:, part * 128:(part + 1) * 128] = grad[part:part + 1, :]
    for k in range(1, 16):
        z_copy(k).wait_send()


def on_device(query_rows, key_rows, value_rows, gate_rows, positives, negatives, history_lengths):
    vmem = pl.BlockSpec(memory_space=pltpu.VMEM)
    hbm = pl.BlockSpec(memory_space=pl.ANY)
    smem = pl.BlockSpec(memory_space=pltpu.SMEM)
    dma = pltpu.SemaphoreType.DMA
    bf16, f32 = jnp.bfloat16, jnp.float32
    return pl.pallas_call(
        kernel,
        out_shape=(
            jax.ShapeDtypeStruct((ROWS, WIDTH), bf16),
            jax.ShapeDtypeStruct((ROWS, WIDTH), bf16),
            jax.ShapeDtypeStruct((1, WIDTH), f32),
        ),
        in_specs=[smem, vmem, hbm, hbm, vmem, vmem, vmem],
        out_specs=(vmem, vmem, vmem),
        scratch_shapes=[
            pltpu.VMEM((4, 4, 2, 4, 2, QUARTER, WIDTH), bf16),
            pltpu.VMEM((ROWS, WIDTH), f32),
            pltpu.VMEM((12, HEADS, ROWS, 8 * QUARTER), f32),
            pltpu.VMEM((4, 2, 4, 16, WIDTH), bf16),
            pltpu.VMEM((512, WIDTH), bf16),
            pltpu.VMEM((ROWS, WIDTH), bf16),
            pltpu.VMEM((256, WIDTH), bf16),
            pltpu.VMEM((256, WIDTH), bf16),
            pltpu.VMEM((256, WIDTH), f32),
            pltpu.VMEM((16, 16, WIDTH), bf16),
            pltpu.VMEM((16, 16, WIDTH), bf16),
            pltpu.VMEM((16, 4, 128), f32),
            pltpu.VMEM((16, 4, 128), f32),
            dma((8,)), dma((4, 4, 4, 2)), dma((2, 2, 4)), dma((12, 3)), dma((12, 4)),
            dma((3,)), dma((1,)), dma((3,)), dma((3,)), dma((3,)), dma((3,)), dma((1,)), dma((1,)),
            dma((1,)), dma((1,)), dma((15,)), dma((15,)), dma((15,)), dma((15,)),
        ],
        name="layer",
        compiler_params=pltpu.CompilerParams(
            collective_id=0, has_side_effects=True, vmem_limit_bytes=48 * 2**20),
    )(history_lengths, query_rows, key_rows, value_rows, gate_rows, positives, negatives)


def solution(mesh):
    rows = P(("dp", "ctx"), None)
    return jax.shard_map(
        on_device,
        mesh=mesh,
        in_specs=(rows, rows, rows, rows, rows, P("dp", None), P("dp", None)),
        out_specs=(rows, rows, rows),
        check_vma=False,
    )
```

time: 709 us -> 99.4 us (0.14)
  waiting for transfers between devices: 598 us -> 0 us
  Pallas kernels: 0 us -> 90.7 us
  blocking collectives: 47.1 us -> 0 us
  matrix products: 21.9 us -> 0 us
  between operations: 13.9 us -> 0.66 us
  local copies, waits for them, and re-layouts: 20.5 us -> 7.81 us
    unnamed x4 -> x0, waiting for transfers between devices: 435 us -> none
    all_gather x2 -> x0, waiting for transfers between devices: 163 us -> none  [the longest x1 102 us: on_device(): lax.all_gather(value_rows, 'ctx', axis=0, tiled=True)]
    pallas_call x0 -> x1, Pallas kernels: none -> 90.7 us  [on_device(): pl.pallas_call(kernel, out_shape=(jax.ShapeDtypeStruct((ROWS, WIDTH), bf1...]
    all_gather x1 -> x0, blocking collectives: 47.1 us -> none  [on_device(): all_negatives = lax.all_gather(negatives, 'dp', axis=0, tiled=True)]
    dot_general x15 -> x0, matrix products: 21.9 us -> none  [the longest x4 12.4 us: add_backward(): jnp.einsum('hrk,khd->rhd', d_logits, k_heads, preferred_element_type=jnp....]
    dynamic_slice x8 -> x0, local copies, waits for them, and re-layouts: 13.8 us -> none  [the longest x4 6.92 us: advance(): k_block = lax.dynamic_slice_in_dim(k_all, offset, block_rows, 0)]
  transfers between devices with their start and end apart: 3 -> 0, of which waited for: 3 -> 0; matrix products, arithmetic and copies ran while one was open for 4% -> 0% of each run, Pallas kernels for 0% -> 0%
where the time goes in v1:
time: 99.4 us; the launch traced here: 99.1 us
  Pallas kernels  90.7 us (91%)
  local copies, waits for them, and re-layouts  7.81 us (8%)
    pallas_call x1, Pallas kernels, on_device(): pl.pallas_call(kernel, out_shape=(jax.ShapeDtypeStruct((ROWS, WIDTH), bf1...  90.7 us
    unnamed x17, local copies, waits for them, and re-layouts  7.81 us

profile of v1, /device:TPU:1, one launch (start us, length us, event | category | flops | bytes accessed | tf_op | source)
XLA Modules:
  0.0 99.1 jit_solution(2301263508107103734)
XLA Ops:
  0.6 0.0 copy-start
  0.6 0.9 copy-done
  1.5 0.0 copy-start.1
  1.5 0.9 copy-done.1
  2.4 0.0 copy-start.2
  2.4 0.9 copy-done.2
  3.3 0.0 copy-start.3
  3.3 0.9 copy-done.3
  4.3 0.0 copy-start.4
  4.3 0.9 copy-done.4
  5.2 0.0 copy-start.5
  5.2 0.8 copy-done.5
  5.9 0.0 copy-start.6
  5.9 0.7 copy-done.6
  6.6 90.7 %layer.1 = (bf16[128,512]{1,0:T(8,128)(2,1)S(1)}, bf16[128,512]{1,0:T(8,128)(2,1)S(1)}, f32[1,512]{1,0:T(1,128)S(1)}) custom-call(s32[1,4]{1,0:T(1,128)S(1)} %copy-done.6, bf16[128,512]{1,0:T(8,128)(2,1)S(1)} %copy-done, bf16[128,512]{1,0:T(8,128)(2,1)S(1)} %copy-done.1, bf16[128,512]{1,0:T(8,128)(2,1)S(1)} %copy-done.2, bf16[128,512]{1,0:T(8,128)(2,1)S(1)} %copy-done.3, ...), custom_call_target="tpu_custom_call" | custom-call | tf_op jit(solution)/shard_map/layer/pallas_call | solution.py:458
  97.2 0.7 copy.13
  97.9 0.7 copy.14
  98.5 0.6 copy.15
Async XLA Ops:
  0.6 0.9 copy-start
  1.5 0.9 copy-start.1
  2.4 0.9 copy-start.2
  3.3 0.9 copy-start.3
  4.3 0.9 copy-start.4
  5.2 0.8 copy-start.5
  5.9 0.7 copy-start.6

commit v2 on v1

--- a/solution.py
+++ b/solution.py
@@ -15,8 +15,21 @@
 MESH = pl.DeviceIdType.MESH
 
 ORDER_1 = (0, 1, 2, 3)
-ORDER_2 = (0, 2, 6, 4, 7, 5, 1, 3)
-ORDER_3 = (0, 1, 4, 5, 2, 6, 3, 7)
+ORDER_2 = (0, 2, 4, 6, 5, 7, 3, 1)
+ORDER_3 = (0, 1, 5, 4, 2, 6, 3, 7)
+
+FORWARD = (
+    ((0, 0), (0, 1), (0, 2), (0, 3), None),
+    ((0, 0), (0, 2), (1, 0), (1, 1), (0, 3)),
+    ((0, 0), (0, 1), (1, 0), (0, 2), (0, 3)),
+    (None,) * 5,
+)
+BACKWARD = (
+    ((0, 2), (0, 3), (-1, 1), (-1, 2), (-1, 3)),
+    ((0, 1), (0, 2), (0, 3), None, None),
+    (None,) * 5,
+    (None, None, (3, 2), (3, 3), (2, 1)),
+)
 
 
 def packed(order):
@@ -43,10 +56,10 @@
 
 
 def kernel(
-    lengths, q_ref, k_hbm, v_hbm, gate_ref, pos_ref, neg_ref,
+    lengths_hbm, q_hbm, k_hbm, v_hbm, gate_hbm, pos_hbm, neg_hbm,
     gq_out, gg_out, gn_out,
-    kv, att, slope, negs_raw, negs, d_att, c_send, c_recv, own_half, xy_send, xy_recv, z_send, z_recv,
-    local_sem, kv_recv, z_sem, y_sem, c_sem,
+    lengths, q_ref, gate_ref, pos_ref, neg_ref, kv, att, slope, negs_raw, negs, d_att, c_send, c_recv, own_half, xy_send, xy_recv, z_send, z_recv,
+    ready_x, ready_z, local_sem, kv_recv, z_sem, y_sem, c_sem,
     nx_send, nx_recv, nl_send, nl_recv, ny_send, ny_recv, nc_send, nc_recv,
     rc_send, rc_recv, rxy_send, rxy_recv, rz_send, rz_recv,
 ):
@@ -73,13 +86,19 @@
         for kind, source in ((0, k_hbm), (1, v_hbm)):
             local.append(pltpu.make_async_copy(
                 source.at[pl.ds(q * QUARTER, QUARTER)], kv.at[h, q, kind, y, c], local_sem.at[q * 2 + kind]))
-    for copy in local:
+    others = []
+    for source, target in (
+        (lengths_hbm, lengths), (neg_hbm, neg_ref), (q_hbm, q_ref), (gate_hbm, gate_ref), (pos_hbm, pos_ref)
+    ):
+        others.append(pltpu.make_async_copy(source, target, local_sem.at[8 + len(others)]))
+    for copy in local + others:
         copy.start()
 
     barrier = pltpu.get_barrier_semaphore()
     pl.semaphore_signal(barrier, inc=1, device_id=sibling, device_id_type=MESH)
-    for k in range(1, 16):
+    for k in (1, 2, 4, 12, 14, 15):
         pl.semaphore_signal(barrier, inc=1, device_id=z_peer(k)[1], device_id_type=MESH)
+    for k in (1, 2, 3, 4, 8, 12):
         pl.semaphore_signal(barrier, inc=1, device_id=xy_peer(k)[1], device_id_type=MESH)
 
     for y2 in range(4):
@@ -96,7 +115,7 @@
     att[...] = jnp.zeros_like(att)
     for copy in local:
         copy.wait()
-    pl.semaphore_wait(barrier, 31)
+    pl.semaphore_wait(barrier, 13)
 
     def piece_copy(hb, q, y2, c2, send_sem, target):
         piece = kv.at[hb, q, :, y2, c2]
@@ -105,24 +124,40 @@
             device_id=target, device_id_type=MESH)
 
     def piece_arrived(hb, q, y2, c2):
-        piece_copy(hb, q, y2, c2, z_sem.at[0, 0, 0], sibling).wait_recv()
-
-    def forward(hb, q, kind):
-        return piece_copy(hb, q, y, c, z_sem.at[0, kind, q], device(x, l, (h + 1) % 4, y, c))
-
-    def backward(hb, q, kind):
-        return piece_copy(hb, q, y, c, z_sem.at[1, kind, q], device(x, l, (h + 3) % 4, y, c))
-
-    def sends_forward(q):
-        return (h <= 2) if q != 1 else ((h == 0) | (h == 2))
-
-    def sends_backward(q):
-        return {0: h < 0, 1: h == 1, 2: h <= 1, 3: h <= 1}[q]
-
-    for q in range(4):
-        pl.when(sends_forward(q))(lambda q=q: forward(h, q, 0).start())
-        if q > 0:
-            pl.when(sends_backward(q))(lambda q=q: backward(h, q, 0).start())
+        piece_copy(hb, q, y2, c2, z_sem.at[0, 0], sibling).wait_recv()
+
+    def z_copy_of(way, number, hh, back, q):
+        target = device(x, l, (hh + (1 if way == 0 else 3)) % 4, y, c)
+        return piece_copy(hh - back, q, y, c, z_sem.at[way, number], target)
+
+    def z_round(number):
+        for way, table in ((0, FORWARD), (1, BACKWARD)):
+            for hh in range(4):
+                @pl.when(h == hh)
+                def _():
+                    earlier = [n for n in range(number) if table[hh][n] is not None]
+                    if table[hh][number] is not None:
+                        back, q = table[hh][number]
+                        if earlier:
+                            z_copy_of(way, earlier[-1], hh, *table[hh][earlier[-1]]).wait_send()
+                        if back in (-1, 3):
+                            piece_arrived(hh - back, q, y, c)
+                        z_copy_of(way, number, hh, back, q).start()
+
+    def z_rounds_left():
+        for way, table in ((0, FORWARD), (1, BACKWARD)):
+            for hh in range(4):
+                used = [n for n in range(5) if table[hh][n] is not None]
+                if used:
+                    last = z_copy_of(way, used[-1], hh, *table[hh][used[-1]])
+                    pl.when(h == hh)(lambda last=last: last.wait_send())
+
+    z_round(0)
+
+    for k in (4, 8, 12):
+        pl.semaphore_signal(ready_x, inc=1, device_id=xy_peer(k)[1], device_id_type=MESH)
+    for k in (4, 12):
+        pl.semaphore_signal(ready_z.at[0], inc=1, device_id=z_peer(k)[1], device_id_type=MESH)
 
     def neg_x(k):
         part = neg_ref.at[pl.ds(c * 16, 16)]
@@ -161,6 +196,9 @@
         return pltpu.make_async_remote_copy(
             src_ref=part, dst_ref=part, send_sem=nc_send.at[0], recv_sem=nc_recv.at[0],
             device_id=sibling, device_id_type=MESH)
+
+    for copy in others:
+        copy.wait()
 
     @pl.when(x == y)
     def _():
@@ -188,28 +226,16 @@
     def goes_to(back, y2):
         return (back == 1) | ((back == 0) & (y2 > y)) | ((back == 2) & (y2 < y))
 
-    def z_forwards(back, q):
-        return ((h == 1) & (back == 1) & (q < 2)) | ((h == 2) & (back == 1) & (q == 0))
-
-    def z_backwards(back, q):
-        return (h == 3) & (back == 2) & (q == 1)
-
     def y_copy(e, hb, q, k):
         return piece_copy(hb, q, y, c, y_sem.at[e, k - 1], device(x, l, h, (y + k) % 4, c))
 
     def c_copy(e, hb, q, y2):
         return piece_copy(hb, q, y2, c, c_sem.at[e, y2], sibling)
-
-    def transit(hb, q):
-        piece_arrived(hb, q, y, c)
-        backward(hb, q, 1).start()
 
     def column_event(e):
         back, q = rank_of(e)
         hb = h - back
         pl.when(back > 0)(lambda: piece_arrived(hb, q, y, c))
-        pl.when(z_forwards(back, q))(lambda: forward(hb, q, 1).start())
-        pl.when(z_backwards(back, q))(lambda: backward(hb, q, 1).start())
         for k in (1, 3, 2):
             pl.when(goes_to(back, (y + k) % 4))(lambda k=k: y_copy(e, hb, q, k).start())
         c_copy(e, hb, q, y).start()
@@ -246,12 +272,13 @@
             att[:, lanes] += dot(weights, v_head)
 
     def step(e, carry):
-        pl.when(e < ranks)(lambda: column_event(e))
-
-        @pl.when(h == 3)
+        pl.when((e >= 4) & (e < ranks))(lambda: column_event(e))
+        pl.when(e == 3)(lambda: z_round(1))
+
+        @pl.when(h != 0)
         def _():
-            pl.when(e == 4)(lambda: transit(0, 2))
-            pl.when(e == 5)(lambda: transit(0, 3))
+            for number in (2, 3, 4):
+                pl.when(e == number + 2)(lambda number=number: z_round(number))
 
         @pl.when(e == 2)
         def _():
@@ -271,6 +298,9 @@
 
         @pl.when(e == 4)
         def _():
+            pl.semaphore_wait(ready_z.at[0], 2)
+            for k in (4, 12):
+                pl.semaphore_signal(ready_z.at[1], inc=1, device_id=z_peer(k)[1], device_id_type=MESH)
             for k in (1, 2, 3):
                 neg_z_arrived(k)
             for k in (1, 2, 3):
@@ -286,15 +316,14 @@
         pl.when((e >= 1) & (e <= ranks))(lambda: row_event(e - 1))
         return carry
 
+    for e in range(4):
+        column_event(e)
+    lax.fori_loop(0, ranks + 2, step, 0)
+
     @pl.when(h == 0)
     def _():
-        lax.fori_loop(0, 6, step, 0)
-        for q in (1, 2, 3):
-            transit(1, q)
-
-    @pl.when(h != 0)
-    def _():
-        lax.fori_loop(0, ranks + 2, step, 0)
+        for number in (2, 3, 4):
+            z_round(number)
 
     neg_c(1 - c).wait_recv()
     to = lax.broadcasted_iota(jnp.int32, (512, 512), 0)
@@ -343,6 +372,7 @@
             src_ref=part, dst_ref=part, send_sem=rxy_send.at[k - 1], recv_sem=rxy_recv.at[k - 1],
             device_id=sibling, device_id_type=MESH).wait_recv()
 
+    pl.semaphore_wait(ready_x, 3)
     for k in range(1, 16):
         xy_copy(k).start()
     xy_recv[here] = xy_send[here]
@@ -391,15 +421,13 @@
             src_ref=part, dst_ref=part, send_sem=rz_send.at[k - 1], recv_sem=rz_recv.at[k - 1],
             device_id=sibling, device_id_type=MESH).wait_recv()
 
+    pl.semaphore_wait(ready_z.at[1], 2)
     for k in (8, 7, 9, 6, 10, 5, 11, 4, 12, 3, 13, 2, 14, 1, 15):
         z_copy(k).start()
     z_recv[z] = z_send[z]
     gq_out[...] = att[...].astype(jnp.bfloat16)
 
-    for q in range(4):
-        pl.when(sends_forward(q))(lambda q=q: forward(h, q, 0).wait_send())
-        if q > 0:
-            pl.when(sends_backward(q))(lambda q=q: backward(h, q, 0).wait_send())
+    z_rounds_left()
 
     @pl.when(x == y)
     def _():
@@ -411,21 +439,9 @@
         neg_y(k).wait_send()
     neg_c(c).wait_send()
 
-    @pl.when(h == 0)
-    def _():
-        for q in (1, 2, 3):
-            backward(1, q, 1).wait_send()
-
-    @pl.when(h == 3)
-    def _():
-        for q in (2, 3):
-            backward(0, q, 1).wait_send()
-
     def drain(e, carry):
         back, q = rank_of(e)
         hb = h - back
-        pl.when(z_forwards(back, q))(lambda: forward(hb, q, 1).wait_send())
-        pl.when(z_backwards(back, q))(lambda: backward(hb, q, 1).wait_send())
         for k in (1, 2, 3):
             y2 = (y + k) % 4
             pl.when(goes_to(back, y2))(lambda k=k: y_copy(e, hb, q, k).wait_send())
@@ -451,8 +467,7 @@
 
 def on_device(query_rows, key_rows, value_rows, gate_rows, positives, negatives, history_lengths):
     vmem = pl.BlockSpec(memory_space=pltpu.VMEM)
-    hbm = pl.BlockSpec(memory_space=pl.ANY)
-    smem = pl.BlockSpec(memory_space=pltpu.SMEM)
+    hbm = pl.BlockSpec(memory_space=pltpu.HBM)
     dma = pltpu.SemaphoreType.DMA
     bf16, f32 = jnp.bfloat16, jnp.float32
     return pl.pallas_call(
@@ -462,9 +477,14 @@
             jax.ShapeDtypeStruct((ROWS, WIDTH), bf16),
             jax.ShapeDtypeStruct((1, WIDTH), f32),
         ),
-        in_specs=[smem, vmem, hbm, hbm, vmem, vmem, vmem],
+        in_specs=[hbm] * 7,
         out_specs=(vmem, vmem, vmem),
         scratch_shapes=[
+            pltpu.SMEM((1, 4), jnp.int32),
+            pltpu.VMEM((ROWS, WIDTH), bf16),
+            pltpu.VMEM((ROWS, WIDTH), bf16),
+            pltpu.VMEM((ROWS, WIDTH), bf16),
+            pltpu.VMEM((32, WIDTH), bf16),
             pltpu.VMEM((4, 4, 2, 4, 2, QUARTER, WIDTH), bf16),
             pltpu.VMEM((ROWS, WIDTH), f32),
             pltpu.VMEM((12, HEADS, ROWS, 8 * QUARTER), f32),
@@ -478,15 +498,15 @@
             pltpu.VMEM((16, 16, WIDTH), bf16),
             pltpu.VMEM((16, 4, 128), f32),
             pltpu.VMEM((16, 4, 128), f32),
-            dma((8,)), dma((4, 4, 4, 2)), dma((2, 2, 4)), dma((12, 3)), dma((12, 4)),
+            pltpu.SemaphoreType.REGULAR, pltpu.SemaphoreType.REGULAR((2,)),
+            dma((13,)), dma((4, 4, 4, 2)), dma((2, 5)), dma((12, 3)), dma((12, 4)),
             dma((3,)), dma((1,)), dma((3,)), dma((3,)), dma((3,)), dma((3,)), dma((1,)), dma((1,)),
             dma((1,)), dma((1,)), dma((15,)), dma((15,)), dma((15,)), dma((15,)),
         ],
         name="layer",
         compiler_params=pltpu.CompilerParams(
-            collective_id=0, has_side_effects=True, vmem_limit_bytes=48 * 2**20),
+            collective_id=0, has_side_effects=True, vmem_limit_bytes=64 * 2**20),
     )(history_lengths, query_rows, key_rows, value_rows, gate_rows, positives, negatives)
-
 
 def solution(mesh):
     rows = P(("dp", "ctx"), None)

time: 99.4 us -> 87.9 us (0.88)
  Pallas kernels: 90.7 us -> 84.1 us
  local copies, waits for them, and re-layouts: 7.81 us -> 2.86 us
    pallas_call x1, Pallas kernels: 90.7 us -> 84.1 us  [on_device(): pl.pallas_call(kernel, out_shape=(jax.ShapeDtypeStruct((ROWS, WIDTH), bf1...]
    unnamed x17 -> x7, local copies, waits for them, and re-layouts: 7.81 us -> 2.86 us
where the time goes in v2:
time: 87.9 us; the launch traced here: 87.6 us
  Pallas kernels  84.1 us (96%)
  local copies, waits for them, and re-layouts  2.86 us (3%)
    pallas_call x1, Pallas kernels, on_device(): pl.pallas_call(kernel, out_shape=(jax.ShapeDtypeStruct((ROWS, WIDTH), bf1...  84.1 us
    unnamed x7, local copies, waits for them, and re-layouts  2.86 us

profile of v2, /device:TPU:1, one launch (start us, length us, event | category | flops | bytes accessed | tf_op | source)
XLA Modules:
  0.0 87.6 jit_solution(8231334979368715117)
XLA Ops:
  0.6 84.1 %layer.1 = (bf16[128,512]{1,0:T(8,128)(2,1)}, bf16[128,512]{1,0:T(8,128)(2,1)}, f32[1,512]{1,0:T(1,128)}) custom-call(s32[1,4]{1,0:T(1,128)} %lengths_hbm.1, bf16[128,512]{1,0:T(8,128)(2,1)} %q_hbm.1, bf16[128,512]{1,0:T(8,128)(2,1)} %k_hbm.1, bf16[128,512]{1,0:T(8,128)(2,1)} %v_hbm.1, bf16[128,512]{1,0:T(8,128)(2,1)} %gate_hbm.1, bf16[128,512]{1,0:T(8,128)(2,1)} %pos_hbm.1, ...), custom_call_target="tpu_custom_call" | custom-call | tf_op jit(solution)/shard_map/layer/pallas_call | solution.py:473
  84.8 0.0 copy-start
  84.8 1.6 %copy.13 = bf16[128,512]{1,0:T(8,128)(2,1)} copy(bf16[128,512]{1,0:T(8,128)(2,1)} %get-tuple-element.6) | data formatting | bytes 262144
  86.4 0.0 copy-done
  86.4 0.0 copy-start.1
  86.4 0.7 copy.14
  87.0 0.0 copy-done.1
  87.0 0.6 copy.15
Async XLA Ops:
  84.8 1.6 %copy-start = (bf16[128,512]{1,0:T(8,128)(2,1)S(1)}, bf16[128,512]{1,0:T(8,128)(2,1)}, u32[]{:S(2)}) copy-start(bf16[128,512]{1,0:T(8,128)(2,1)} %get-tuple-element.7) | copy-start | bytes 393220
  86.4 0.7 copy-start.1
